TPU v7x, 32 devices: a whole 2x2x4 slice. The times are simulated.
32 devices in a mesh: uvrow: 4 (over z), chan: 2 (over y), tm: 4 (over x, core).
Axes of the slice: x: 2, y: 2, z: 4, core: 2. Of those that a mesh axis runs over, the one named last changes fastest.
Arguments:
- residual_visibility: float32 [2, 32, 128, 8192], P(None, 'tm', 'chan', 'uvrow'), may hold values from -6 to 6
- noise_weight: float32 [32, 128, 8192], P('tm', 'chan', 'uvrow'), may hold values from 0.2 to 5
- uv_tile: int32 [8192, 1], P('uvrow'), may hold values from 0 to 15; in each aligned block of 2048 rows (0 to 2047, 2048 to 4095, ...) at most 256 rows name the same one
- row_offset: int32 [8192], P('uvrow'), may hold values from 0 to 15
- col_offset: int32 [8192], P('uvrow'), may hold values from 0 to 255
- kernel_u: float32 [8, 8192], P(None, 'uvrow'), may hold values from 0.1 to 1
- kernel_v: float32 [8, 8192], P(None, 'uvrow'), may hold values from 0.1 to 1
- sky_model: float32 [128, 256, 256], P('chan', ('uvrow', 'tm')), may hold values from -6 to 6
- prior_precision: float32 [128, 256, 256], P('chan', ('uvrow', 'tm')), may hold values from 0.1 to 3
Outputs:
- gradient: float32 [128, 256, 256], P('chan', ('uvrow', 'tm'))
Inputs may be any that keep to these rules, and one draw needn't show every extreme that they name: `uv_tile`: among the 2048 baselines of one index of uvrow (an aligned block), at most 256 name the same tile, a bound that some block reaches.
All inputs are finite; a program needn't handle non-finite values.
Results may differ from a plain program's by a relative error of at most 0.000064.
Values sent between devices are 32-bit elements; how exact they have to be, the bound alone decides.
A program may use at most 64 MiB of HBM per device.

v0:
```python
import functools
import math

import jax
import jax.numpy as jnp
import numpy as np
from jax import lax
from jax.experimental import pallas as pl
from jax.experimental.pallas import tpu as pltpu
from jax.sharding import PartitionSpec as P

NU = 256
NV = 256
KER = 8
PAD = 8
HALF = NU // 2 + 2 * PAD
MESH = pl.DeviceIdType.MESH


def split3(table, axis):
    high = table.astype(jnp.bfloat16)
    low = (table - high.astype(np.float64)).astype(jnp.bfloat16)
    return np.concatenate([high, high, low], axis=axis)


def tables():
    rows = np.arange(HALF) - PAD
    modes = np.arange(NU)
    angle_u = 2.0 * np.pi / NU * ((modes[:, None] * rows[None, :]) % NU)
    cos_u, sin_u = np.cos(angle_u), np.sin(angle_u)
    table_u = np.concatenate(
        [np.concatenate([cos_u, -sin_u], 1), np.concatenate([sin_u, cos_u], 1)], 0
    )
    angle_v = 2.0 * np.pi / NV * ((np.arange(NV)[:, None] * np.arange(NV)[None, :]) % NV)
    table_v = np.concatenate([np.cos(angle_v), -np.sin(angle_v)], 1)
    return split3(table_u, 1), split3(table_v, 1)


def parts(values):
    high = values.astype(jnp.bfloat16)
    return high, (values - high.astype(jnp.float32)).astype(jnp.bfloat16)


def taps(offset, sign, kernel, count, first):
    length = offset.shape[1]
    lane8 = lax.broadcasted_iota(jnp.int32, (KER, length), 0)
    index = (sign * lane8 - offset) & (KER - 1)
    turned = jnp.zeros((KER, length), jnp.float32)
    for j in range(KER):
        turned = jnp.where(index == j, kernel[j : j + 1], turned)
    place = lax.broadcasted_iota(jnp.int32, (count, length), 0) + first
    return jnp.concatenate([turned] * (count // KER), axis=0), sign * place - offset


def fit_kernel(
    nz, nt, own, chunk, scale,
    res_hbm, weight_hbm, ku_ref, kv_ref, tile_ref, row_ref, col_ref, tu_ref, tv_ref,
    out_ref,
    res, weight, part, got_a, got_b, mixed, vis, ku, kv, off, rows, cols, wide_a, wide_b, acc, image,
    load_sem, send_a, recv_a, send_b, recv_b, send_c, recv_c, send_k, recv_k, send_o, recv_o, send_i, recv_i, local_sem,
):
    z = lax.axis_index("uvrow")
    q = lax.axis_index("tm")
    half = nt // 2
    high, core = q // 2, lax.rem(q, 2)
    count = nz * nt
    me = z * nt + q
    modes = NV // count
    length = res.shape[3]
    per = length // chunk
    chunks = nz * per
    group = 8
    per_z = nt * own // group
    pairs = group // (2 * own)
    at_z = [lax.rem(z + 1 + k, nz) for k in range(nz)]

    loads = []
    for n in range(nz * per_z):
        first = pl.multiple_of((at_z[n // per_z] * per_z + n % per_z) * group, group)
        at = pl.ds(first, group)
        pair = [
            pltpu.make_async_copy(res_hbm.at[:, :, at], res.at[:, :, pl.ds(n * group, group)], load_sem.at[n, 0]),
            pltpu.make_async_copy(weight_hbm.at[:, at], weight.at[:, pl.ds(n * group, group)], load_sem.at[n, 1]),
        ]
        for copy in pair:
            copy.start()
        loads.append(pair)

    def device(i):
        peer = lax.rem(me + i, count)
        return peer, {"uvrow": peer // nt, "tm": lax.rem(peer, nt)}

    barrier = pltpu.get_barrier_semaphore()
    for i in range(1, count):
        pl.semaphore_signal(barrier, inc=1, device_id=device(i)[1], device_id_type=MESH)
    off[z, 0:1] = tile_ref[...] * (NU // count) + row_ref[...]
    off[z, 1:2] = col_ref[...]
    ku[z] = ku_ref[...]
    kv[z] = kv_ref[...]
    pl.semaphore_wait(barrier, count - 1)

    def to_z(k, source, target, send, recv):
        return pltpu.make_async_remote_copy(
            source, target, send, recv, device_id={"uvrow": at_z[k]}, device_id_type=MESH
        )

    kernels = []
    for k in range(nz - 1):
        kernels.append(
            [
                to_z(k, off.at[z], off.at[z], send_o.at[k], recv_o.at[k]),
                to_z(k, ku.at[z], ku.at[z], send_k.at[k, 0], recv_k.at[k, 0]),
                to_z(k, kv.at[z], kv.at[z], send_k.at[k, 1], recv_k.at[k, 1]),
            ]
        )
        for copy in kernels[k]:
            copy.start()

    halves = []
    for n in range(nz * per_z):
        for copy in loads[n]:
            copy.wait()
        at = slice(n * group, (n + 1) * group)
        total = [res[p, 0, at] * weight[0, at] for p in range(2)]
        for t in range(1, res.shape[1]):
            total = [total[p] + res[p, t, at] * weight[t, at] for p in range(2)]
        for j in range(2 * pairs):
            for p in range(2):
                part[n * pairs + j // 2, j % 2, p * own : (p + 1) * own] = (
                    total[p][j * own : (j + 1) * own] * scale
                )
        where = pl.ds(n * pairs, pairs)
        copy = pltpu.make_async_remote_copy(
            part.at[where, 1 - core], got_a.at[where], send_a.at[n], recv_a.at[n],
            device_id={"tm": high * 2 + 1 - core}, device_id_type=MESH,
        )
        copy.start()
        halves.append(copy)

    quarters = []
    for k in range(nz):
        for s in range(per_z):
            halves[k * per_z + s].wait()
        for h in range(half):
            mixed[k, h] = part[k * half + h, core] + got_a[k * half + h]
        for i in range(1, half):
            to = lax.rem(high + i, half)
            copy = pltpu.make_async_remote_copy(
                mixed.at[k, to], got_b.at[k, i - 1], send_b.at[k, i - 1], recv_b.at[k, i - 1],
                device_id={"tm": to * 2 + core}, device_id_type=MESH,
            )
            copy.start()
            quarters.append(copy)

    def tabulate(at):
        def one(k, carry):
            lanes = pl.ds(pl.multiple_of(k * chunk, chunk), chunk)
            start = off[at, 0:1, lanes]
            column = off[at, 1:2, lanes]
            flipped = start >= NU // 2
            sign = jnp.where(flipped, -1, 1)
            start = jnp.where(flipped, start - NU, start)
            values, tap = taps(column, sign, kv[at, :, lanes], NV, 0)
            v_high, v_low = parts(jnp.where((tap & (NV - 1)) < KER, values, 0.0))
            n = at * per + k
            cols[n, :, :chunk] = v_high
            cols[n, :, chunk : 2 * chunk] = v_low
            cols[n, :, 2 * chunk :] = v_high
            values, tap = taps(start, sign, ku[at, :, lanes], HALF, -PAD)
            rows[n] = jnp.where((tap >= 0) & (tap < KER), values, 0.0)
            return carry

        lax.fori_loop(0, per, one, 0)

    tabulate(z)
    blocks = []
    for k in range(nz):
        for i in range(half - 1):
            quarters[k * (half - 1) + i].wait()
        total = mixed[k, high]
        for i in range(half - 1):
            total = total + got_b[k, i]
        if k == nz - 1:
            vis[z] = total
            continue
        part[k, 0] = total
        copy = to_z(k, part.at[k, 0], vis.at[z], send_c.at[k], recv_c.at[k])
        copy.start()
        blocks.append(copy)
    for k in range(nz - 1):
        for copy in kernels[k]:
            copy.wait()
    for k in range(nz - 1):
        tabulate(at_z[k])
    for copy in blocks:
        copy.wait()

    def build(n, wide):
        f, c = n // chunks, lax.rem(n, chunks)
        lanes = pl.ds(pl.multiple_of(lax.rem(c, per) * chunk, chunk), chunk)
        table = rows[c]
        sign = jnp.where(off[c // per, 0:1, lanes] >= NU // 2, -1.0, 1.0)
        for p in range(2):
            row = vis[c // per, pl.ds(p * own + f, 1), lanes]
            if p:
                row = row * sign
            w_high, w_low = parts(table * row)
            at = slice(p * HALF, (p + 1) * HALF)
            wide[at, :chunk] = w_high
            wide[at, chunk : 2 * chunk] = w_high
            wide[at, 2 * chunk :] = w_low

    def product(wide, c):
        return lax.dot_general(
            wide[...], cols[c], (((1,), (1,)), ((), ())), preferred_element_type=jnp.float32
        )

    def send(f, i):
        peer, to = device(i)
        return pltpu.make_async_remote_copy(
            image.at[f, pl.ds(pl.multiple_of(peer * modes, modes), modes)], out_ref.at[me * own + f],
            send_i.at[f, i], recv_i.at[f, i], device_id=to, device_id_type=MESH,
        )

    def keep(f):
        return pltpu.make_async_copy(
            image.at[f, pl.ds(pl.multiple_of(me * modes, modes), modes)], out_ref.at[me * own + f], local_sem.at[f]
        )

    build(0, wide_a)

    def channel(f, carry):
        acc[...] = jnp.zeros_like(acc)

        def two(k, carry):
            n = f * chunks + 2 * k
            build(n + 1, wide_b)
            acc[...] += product(wide_a, 2 * k)
            build(lax.rem(n + 2, own * chunks), wide_a)
            acc[...] += product(wide_b, 2 * k + 1)
            return carry

        lax.fori_loop(0, chunks // 2, two, 0)
        g_high, g_low = parts(acc[...])
        turned = jnp.dot(
            tu_ref[...],
            jnp.concatenate([g_high, g_low, g_high], axis=0),
            preferred_element_type=jnp.float32,
        )
        g_high, g_low = parts(jnp.concatenate([turned[:NU], turned[NU:]], axis=1))
        image[f] = lax.dot_general(
            tv_ref[...],
            jnp.concatenate([g_high, g_low, g_high], axis=1),
            (((1,), (1,)), ((), ())),
            preferred_element_type=jnp.float32,
        )
        for i in range(1, count):
            send(f, i).start()
        keep(f).start()
        return carry

    lax.fori_loop(0, own, channel, 0)

    def finish(f, carry):
        for i in range(1, count):
            send(f, i).wait()
        keep(f).wait()
        return carry

    lax.fori_loop(0, own, finish, 0)


def body(
    residual_visibility,
    noise_weight,
    uv_tile,
    row_offset,
    col_offset,
    kernel_u,
    kernel_v,
    sky_model,
    prior_precision,
):
    nz = lax.axis_size("uvrow")
    nt = lax.axis_size("tm")
    count = nz * nt
    times = residual_visibility.shape[1]
    channels = residual_visibility.shape[2]
    length = residual_visibility.shape[3]
    own = channels // count
    half = nt // 2
    scale = 1.0 / (KER * math.sqrt(times * nt * length * nz))
    f32 = jnp.float32
    bf16 = jnp.bfloat16
    chunk = min(512, length)
    chunks = nz * (length // chunk)
    table_u, table_v = tables()
    dma = pltpu.SemaphoreType.DMA
    vmem = pltpu.VMEM
    in_vmem = pl.BlockSpec(memory_space=pltpu.VMEM)
    in_hbm = pl.BlockSpec(memory_space=pl.ANY)
    groups = channels // 8

    sky_image = pl.pallas_call(
        functools.partial(fit_kernel, nz, nt, own, chunk, scale),
        in_specs=[in_hbm] * 2 + [in_vmem] * 7,
        out_specs=in_hbm,
        out_shape=jax.ShapeDtypeStruct(sky_model.shape, f32),
        scratch_shapes=[
            vmem((2, times, channels, length), f32),
            vmem((times, channels, length), f32),
            vmem((count // 2, 2, 2 * own, length), f32),
            vmem((count // 2, 2 * own, length), f32),
            vmem((nz, half - 1, 2 * own, length), f32),
            vmem((nz, half, 2 * own, length), f32),
            vmem((nz, 2 * own, length), f32),
            vmem((nz, KER, length), f32),
            vmem((nz, KER, length), f32),
            vmem((nz, 2, length), jnp.int32),
            vmem((chunks, HALF, chunk), f32),
            vmem((chunks, NV, 3 * chunk), bf16),
            vmem((2 * HALF, 3 * chunk), bf16),
            vmem((2 * HALF, 3 * chunk), bf16),
            vmem((2 * HALF, NV), f32),
            vmem((own, NV, NU), f32),
            dma((groups, 2)),
            dma((groups,)), dma((groups,)),
            dma((nz, half - 1)), dma((nz, half - 1)),
            dma((nz - 1,)), dma((nz - 1,)),
            dma((nz - 1, 2)), dma((nz - 1, 2)),
            dma((nz - 1,)), dma((nz - 1,)),
            dma((own, count)), dma((own, count)),
            dma((own,)),
        ],
        compiler_params=pltpu.CompilerParams(
            collective_id=0, has_side_effects=True, vmem_limit_bytes=58 * 1024 * 1024
        ),
    )(
        residual_visibility,
        noise_weight,
        kernel_u,
        kernel_v,
        uv_tile.reshape(1, length),
        row_offset.reshape(1, length),
        col_offset.reshape(1, length),
        jnp.asarray(table_u),
        jnp.asarray(table_v),
    )
    return sky_image - prior_precision * sky_model


def solution(mesh):
    return jax.shard_map(
        body,
        mesh=mesh,
        in_specs=(
            P(None, "tm", "chan", "uvrow"),
            P("tm", "chan", "uvrow"),
            P("uvrow", None),
            P("uvrow"),
            P("uvrow"),
            P(None, "uvrow"),
            P(None, "uvrow"),
            P("chan", ("uvrow", "tm"), None),
            P("chan", ("uvrow", "tm"), None),
        ),
        out_specs=P("chan", ("uvrow", "tm"), None),
        check_vma=False,
    )
```

profile of v0, /device:TPU:11, one launch (start us, length us, event | category | flops | bytes accessed | tf_op | source)
XLA Modules:
  0.0 62.6 jit_solution(5406378955330301575)
XLA Ops:
  0.0 0.0 copy-start
  0.0 0.0 copy-start.1
  0.0 60.0 %shard_map.109 = f32[64,16,256]{2,1,0:T(8,128)} custom-call(f32[2,8,64,2048]{3,2,1,0:T(8,128)} %res_hbm.1, f32[8,64,2048]{2,1,0:T(8,128)} %weight_hbm.1, f32[8,2048]{1,0:T(8,128)} %ku_ref.1, f32[8,2048]{1,0:T(8,128)} %kv_ref.1, s32[1,2048]{1,0:T(1,128)} %bitcast.3, s32[1,2048]{1,0:T(1,128)} %bitcast.4, s32[1,2048]{1,0:T(1,128)} %bitcast.5, ...), custom_call_target="tpu_custom_call" | custom-call | tf_op jit(solution)/shard_map/pallas_call | solution.py:304
  60.1 0.0 copy-done
  60.1 0.0 copy-done.1
  60.1 2.5 %multiply_subtract_fusion = f32[64,16,256]{2,1,0:T(8,128)} fusion(f32[64,16,256]{2,1,0:T(8,128)} %shard_map.109, f32[64,16,256]{2,1,0:T(8,128)S(1)} %copy-done, f32[64,16,256]{2,1,0:T(8,128)S(1)} %copy-done.1), kind=kLoop, calls=%fused_computation | loop fusion | flops 524288 | bytes 4194304 | tf_op jit(solution)/shard_map/sub | solution.py:349
Async XLA Ops:
  0.0 60.1 %copy-start = (f32[64,16,256]{2,1,0:T(8,128)S(1)}, f32[64,16,256]{2,1,0:T(8,128)}, u32[]{:S(2)}) copy-start(f32[64,16,256]{2,1,0:T(8,128)} %param.19) | copy-start | bytes 3145732
  0.0 60.1 %copy-start.1 = (f32[64,16,256]{2,1,0:T(8,128)S(1)}, f32[64,16,256]{2,1,0:T(8,128)}, u32[]{:S(2)}) copy-start(f32[64,16,256]{2,1,0:T(8,128)} %param.18) | copy-start | bytes 3145732
where the time goes:
time: 63.6 us; the launch traced here: 62.6 us
  Pallas kernels  60 us (94%)
  other arithmetic  2.54 us (4%)
    pallas_call x1, Pallas kernels, body(): pl.pallas_call(functools.partial(fit_kernel, nz, nt, own, chunk, scale),...  60 us
    sub x1, other arithmetic, body(): return sky_image - prior_precision * sky_model  2.54 us

commit v1 on v0

--- a/solution.py
+++ b/solution.py
@@ -67,6 +67,7 @@
     me = z * nt + q
     modes = NV // count
     length = res.shape[3]
+    batch = 2 if own % 2 == 0 else 1
     per = length // chunk
     chunks = nz * per
     group = 8
@@ -116,8 +117,9 @@
         for copy in kernels[k]:
             copy.start()
 
-    halves = []
-    for n in range(nz * per_z):
+    halves, quarters, blocks = [], [], []
+
+    def add_times(n):
         for copy in loads[n]:
             copy.wait()
         at = slice(n * group, (n + 1) * group)
@@ -137,8 +139,7 @@
         copy.start()
         halves.append(copy)
 
-    quarters = []
-    for k in range(nz):
+    def add_cores(k):
         for s in range(per_z):
             halves[k * per_z + s].wait()
         for h in range(half):
@@ -151,6 +152,20 @@
             )
             copy.start()
             quarters.append(copy)
+
+    def add_chips(k):
+        for i in range(half - 1):
+            quarters[k * (half - 1) + i].wait()
+        total = mixed[k, high]
+        for i in range(half - 1):
+            total = total + got_b[k, i]
+        if k == nz - 1:
+            vis[z] = total
+            return
+        part[k, 0] = total
+        copy = to_z(k, part.at[k, 0], vis.at[z], send_c.at[k], recv_c.at[k])
+        copy.start()
+        blocks.append(copy)
 
     def tabulate(at):
         def one(k, carry):
@@ -172,21 +187,17 @@
 
         lax.fori_loop(0, per, one, 0)
 
+    for k in range(nz):
+        for s in range(per_z):
+            add_times(k * per_z + s)
+        if k >= 1:
+            add_cores(k - 1)
+        if k >= 2:
+            add_chips(k - 2)
+    add_cores(nz - 1)
+    add_chips(nz - 2)
     tabulate(z)
-    blocks = []
-    for k in range(nz):
-        for i in range(half - 1):
-            quarters[k * (half - 1) + i].wait()
-        total = mixed[k, high]
-        for i in range(half - 1):
-            total = total + got_b[k, i]
-        if k == nz - 1:
-            vis[z] = total
-            continue
-        part[k, 0] = total
-        copy = to_z(k, part.at[k, 0], vis.at[z], send_c.at[k], recv_c.at[k])
-        copy.start()
-        blocks.append(copy)
+    add_chips(nz - 1)
     for k in range(nz - 1):
         for copy in kernels[k]:
             copy.wait()
@@ -196,16 +207,16 @@
         copy.wait()
 
     def build(n, wide):
-        f, c = n // chunks, lax.rem(n, chunks)
+        f, c = n // chunks * batch, lax.rem(n, chunks)
         lanes = pl.ds(pl.multiple_of(lax.rem(c, per) * chunk, chunk), chunk)
         table = rows[c]
         sign = jnp.where(off[c // per, 0:1, lanes] >= NU // 2, -1.0, 1.0)
-        for p in range(2):
-            row = vis[c // per, pl.ds(p * own + f, 1), lanes]
-            if p:
+        for e in range(2 * batch):
+            row = vis[c // per, pl.ds(e % 2 * own + f + e // 2, 1), lanes]
+            if e % 2:
                 row = row * sign
             w_high, w_low = parts(table * row)
-            at = slice(p * HALF, (p + 1) * HALF)
+            at = slice(e * HALF, (e + 1) * HALF)
             wide[at, :chunk] = w_high
             wide[at, chunk : 2 * chunk] = w_high
             wide[at, 2 * chunk :] = w_low
@@ -229,37 +240,39 @@
 
     build(0, wide_a)
 
-    def channel(f, carry):
+    def channels(g, carry):
         acc[...] = jnp.zeros_like(acc)
 
         def two(k, carry):
-            n = f * chunks + 2 * k
+            n = g * chunks + 2 * k
             build(n + 1, wide_b)
             acc[...] += product(wide_a, 2 * k)
-            build(lax.rem(n + 2, own * chunks), wide_a)
+            build(lax.rem(n + 2, own // batch * chunks), wide_a)
             acc[...] += product(wide_b, 2 * k + 1)
             return carry
 
         lax.fori_loop(0, chunks // 2, two, 0)
-        g_high, g_low = parts(acc[...])
-        turned = jnp.dot(
-            tu_ref[...],
-            jnp.concatenate([g_high, g_low, g_high], axis=0),
-            preferred_element_type=jnp.float32,
-        )
-        g_high, g_low = parts(jnp.concatenate([turned[:NU], turned[NU:]], axis=1))
-        image[f] = lax.dot_general(
-            tv_ref[...],
-            jnp.concatenate([g_high, g_low, g_high], axis=1),
-            (((1,), (1,)), ((), ())),
-            preferred_element_type=jnp.float32,
-        )
-        for i in range(1, count):
-            send(f, i).start()
-        keep(f).start()
+        for e in range(batch):
+            f = g * batch + e
+            g_high, g_low = parts(acc[2 * e * HALF : 2 * (e + 1) * HALF])
+            turned = jnp.dot(
+                tu_ref[...],
+                jnp.concatenate([g_high, g_low, g_high], axis=0),
+                preferred_element_type=jnp.float32,
+            )
+            g_high, g_low = parts(jnp.concatenate([turned[:NU], turned[NU:]], axis=1))
+            image[f] = lax.dot_general(
+                tv_ref[...],
+                jnp.concatenate([g_high, g_low, g_high], axis=1),
+                (((1,), (1,)), ((), ())),
+                preferred_element_type=jnp.float32,
+            )
+            for i in range(1, count):
+                send(f, i).start()
+            keep(f).start()
         return carry
 
-    lax.fori_loop(0, own, channel, 0)
+    lax.fori_loop(0, own // batch, channels, 0)
 
     def finish(f, carry):
         for i in range(1, count):
@@ -289,6 +302,7 @@
     length = residual_visibility.shape[3]
     own = channels // count
     half = nt // 2
+    batch = 2 if own % 2 == 0 else 1
     scale = 1.0 / (KER * math.sqrt(times * nt * length * nz))
     f32 = jnp.float32
     bf16 = jnp.bfloat16
@@ -319,9 +333,9 @@
             vmem((nz, 2, length), jnp.int32),
             vmem((chunks, HALF, chunk), f32),
             vmem((chunks, NV, 3 * chunk), bf16),
-            vmem((2 * HALF, 3 * chunk), bf16),
-            vmem((2 * HALF, 3 * chunk), bf16),
-            vmem((2 * HALF, NV), f32),
+            vmem((2 * batch * HALF, 3 * chunk), bf16),
+            vmem((2 * batch * HALF, 3 * chunk), bf16),
+            vmem((2 * batch * HALF, NV), f32),
             vmem((own, NV, NU), f32),
             dma((groups, 2)),
             dma((groups,)), dma((groups,)),

time: 63.6 us -> 64.2 us (level)
  Pallas kernels: 60 us -> 60.7 us
where the time goes in v1:
time: 64.2 us; the launch traced here: 63.2 us
  Pallas kernels  60.7 us (95%)
  other arithmetic  2.54 us (4%)
    pallas_call x1, Pallas kernels, body(): pl.pallas_call(functools.partial(fit_kernel, nz, nt, own, chunk, scale),...  60.7 us
    sub x1, other arithmetic, body(): return sky_image - prior_precision * sky_model  2.54 us

profile of v1, /device:TPU:11, one launch (start us, length us, event | category | flops | bytes accessed | tf_op | source)
XLA Modules:
  0.0 63.2 jit_solution(5667497642042879391)
XLA Ops:
  0.0 0.0 copy-start
  0.0 0.0 copy-start.1
  0.0 60.7 %shard_map.109 = f32[64,16,256]{2,1,0:T(8,128)} custom-call(f32[2,8,64,2048]{3,2,1,0:T(8,128)} %res_hbm.1, f32[8,64,2048]{2,1,0:T(8,128)} %weight_hbm.1, f32[8,2048]{1,0:T(8,128)} %ku_ref.1, f32[8,2048]{1,0:T(8,128)} %kv_ref.1, s32[1,2048]{1,0:T(1,128)} %bitcast.3, s32[1,2048]{1,0:T(1,128)} %bitcast.4, s32[1,2048]{1,0:T(1,128)} %bitcast.5, ...), custom_call_target="tpu_custom_call" | custom-call | tf_op jit(solution)/shard_map/pallas_call | solution.py:318
  60.7 0.0 copy-done
  60.7 0.0 copy-done.1
  60.7 2.5 %multiply_subtract_fusion = f32[64,16,256]{2,1,0:T(8,128)} fusion(f32[64,16,256]{2,1,0:T(8,128)} %shard_map.109, f32[64,16,256]{2,1,0:T(8,128)S(1)} %copy-done, f32[64,16,256]{2,1,0:T(8,128)S(1)} %copy-done.1), kind=kLoop, calls=%fused_computation | loop fusion | flops 524288 | bytes 4194304 | tf_op jit(solution)/shard_map/sub | solution.py:363
Async XLA Ops:
  0.0 60.7 %copy-start = (f32[64,16,256]{2,1,0:T(8,128)S(1)}, f32[64,16,256]{2,1,0:T(8,128)}, u32[]{:S(2)}) copy-start(f32[64,16,256]{2,1,0:T(8,128)} %param.19) | copy-start | bytes 3145732
  0.0 60.7 %copy-start.1 = (f32[64,16,256]{2,1,0:T(8,128)S(1)}, f32[64,16,256]{2,1,0:T(8,128)}, u32[]{:S(2)}) copy-start(f32[64,16,256]{2,1,0:T(8,128)} %param.18) | copy-start | bytes 3145732
